TPU v7x, 32 devices: a whole 2x2x4 slice. The times are simulated.
32 devices in a mesh: facet: 4 (over x, core), band: 8 (over z, y).
Axes of the slice: x: 2, y: 2, z: 4, core: 2. Of those that a mesh axis runs over, the one named last changes fastest.
Arguments:
- visibilities: bfloat16 [4, 4, 128, 2, 256], P('facet', None, 'band'), may hold values from -6 to 6
- uv_coords: float32 [4, 4, 2, 256], replicated, may hold values from -12 to 12
- aterms: bfloat16 [4, 4, 4, 2, 1024], P('facet'), may hold values from -5 to 5
- offsets: int32 [4, 4, 2, 4], P('facet'), may hold values from 0 to 2016
- counts: int32 [4, 4], P('facet'), may hold values from 1 to 4, as said below
- owner: int32 [4], replicated, may hold values from 0 to 3, as said below
Outputs:
- facet_tiles: float32 [4, 2, 2048, 2048], P('facet', None, 'band')
Inputs may be any that keep to these rules, and one draw needn't show every extreme that they name: `owner`: each facet index appears exactly once. `counts`: some entry equals 4.
All inputs are finite; a program needn't handle non-finite values.
Results may differ from a plain program's by a relative error of at most 0.0036.
Values may be sent and summed in bfloat16 or wider, within the bound.
A program may use at most 64 MiB of HBM per device.

v0:
```python
import math

import jax
import jax.numpy as jnp
from jax import lax
from jax.sharding import PartitionSpec as P

NPIX = 32
TILE = 2048


TWO_PI = 2.0 * math.pi


def spread(block, axis, holder):
    block = jnp.where(lax.axis_index(axis) == holder, block, jnp.zeros_like(block))
    return lax.psum(block, axis)


def dft_tables(side_pix):
    pixel_index = jnp.arange(side_pix, dtype=jnp.int32)
    phase_turns = pixel_index[:, None] * pixel_index[None, :] % side_pix
    dft_angle = TWO_PI * phase_turns.astype(jnp.float32) / side_pix
    return (jnp.cos(dft_angle), jnp.sin(dft_angle))


def subgrid_image(vis_block, coords, chan_freq, pixel_pos, facet_shift):
    side_pix = pixel_pos.shape[0]
    u_coord = (coords[0][None, :] * chan_freq[:, None]).reshape(-1)
    v_coord = (coords[1][None, :] * chan_freq[:, None]).reshape(-1)
    vis_real = vis_block[:, 0, :].reshape(-1).astype(jnp.float32)
    vis_imag = vis_block[:, 1, :].reshape(-1).astype(jnp.float32)
    angle_left = TWO_PI * (pixel_pos + facet_shift)[:, None] * u_coord[None, :]
    cos_left = jnp.cos(angle_left)
    sin_left = jnp.sin(angle_left)
    left_ops = jnp.concatenate(
        [cos_left * vis_real - sin_left * vis_imag, sin_left * vis_real + cos_left * vis_imag],
        axis=0,
    ).astype(jnp.bfloat16)
    angle_right = TWO_PI * pixel_pos[:, None] * v_coord[None, :]
    right_ops = jnp.concatenate([jnp.cos(angle_right), jnp.sin(angle_right)], axis=0).astype(
        jnp.bfloat16
    )
    product = lax.dot_general(
        left_ops, right_ops, (((1,), (1,)), ((), ())), preferred_element_type=jnp.float32
    )
    image_re = product[:side_pix, :side_pix] - product[side_pix:, side_pix:]
    image_im = product[:side_pix, side_pix:] + product[side_pix:, :side_pix]
    return jnp.stack([image_re.reshape(-1), image_im.reshape(-1)])


def image_to_grid(image, aterm_vals, live_weight, dft_cos, dft_sin):
    side_pix = dft_cos.shape[0]
    image_re = image[0].reshape(side_pix, side_pix)
    image_im = image[1].reshape(side_pix, side_pix)
    gains = aterm_vals.astype(jnp.float32).reshape(2, side_pix, side_pix)
    weighted_re = (image_re * gains[0] - image_im * gains[1]) * live_weight
    weighted_im = (image_re * gains[1] + image_im * gains[0]) * live_weight
    highest = lax.Precision.HIGHEST
    half_re = jnp.dot(dft_cos, weighted_re, precision=highest) + jnp.dot(
        dft_sin, weighted_im, precision=highest
    )
    half_im = jnp.dot(dft_cos, weighted_im, precision=highest) - jnp.dot(
        dft_sin, weighted_re, precision=highest
    )
    grid_re = jnp.dot(half_re, dft_cos, precision=highest) + jnp.dot(
        half_im, dft_sin, precision=highest
    )
    grid_im = jnp.dot(half_im, dft_cos, precision=highest) - jnp.dot(
        half_re, dft_sin, precision=highest
    )
    return jnp.stack([grid_re, grid_im])


def body(visibilities, uv_coords, aterms, offsets, counts, owner):
    facet_count = lax.axis_size("facet")
    band_count = lax.axis_size("band")
    facet_id = lax.axis_index("facet")
    band_id = lax.axis_index("band")
    sub_count = visibilities.shape[1]
    chan_local = visibilities.shape[2]
    row_count = visibilities.shape[4]
    step_count = owner.shape[0]
    side_pix = NPIX
    tile_side = TILE
    chan_total = chan_local * band_count
    step_order = jnp.arange(step_count, dtype=jnp.int32)
    same_owner = (owner[None, :] == owner[:, None]) & (step_order[None, :] < step_order[:, None])
    earlier = jnp.sum(same_owner.astype(jnp.int32), axis=1)
    chan_index = band_id * chan_local + jnp.arange(chan_local, dtype=jnp.int32)
    chan_freq = 1.0 + 0.5 * chan_index.astype(jnp.float32) / chan_total
    pixel_pos = (jnp.arange(side_pix, dtype=jnp.int32) - side_pix // 2).astype(
        jnp.float32
    ) / side_pix
    facet_shift = (facet_id.astype(jnp.float32) + 0.5) / facet_count - 0.5
    dft_cos, dft_sin = dft_tables(side_pix)
    norm_scale = 1.0 / (side_pix * math.sqrt(row_count * chan_total))

    def advance(carry, step_index):
        own_block = lax.dynamic_index_in_dim(visibilities, earlier[step_index], 0, keepdims=False)
        vis_block = spread(own_block, "facet", owner[step_index])
        coords = lax.dynamic_index_in_dim(uv_coords, step_index, 0, keepdims=False)
        images = [
            subgrid_image(vis_block[subgrid], coords[subgrid], chan_freq, pixel_pos, facet_shift)
            for subgrid in range(sub_count)
        ]
        return (carry, jnp.stack(images))

    unused, image_stack = lax.scan(advance, jnp.zeros((), jnp.int32), step_order)
    total_subs = step_count * sub_count
    image_stack = image_stack.reshape(total_subs, 2, side_pix * side_pix)
    gain_stack = aterms[0].reshape(total_subs, 2, side_pix * side_pix)
    live_index = jnp.arange(sub_count, dtype=jnp.int32)[None, :] < counts[0][:, None]
    weight_stack = jnp.where(live_index, norm_scale, 0.0).astype(jnp.float32).reshape(total_subs)

    def to_grid(image, gain, weight):
        return image_to_grid(image, gain, weight, dft_cos, dft_sin)

    local_grids = jax.vmap(to_grid)(image_stack, gain_stack, weight_stack)
    grid_stack = lax.psum(local_grids, "band")
    band_rows = tile_side // band_count
    row_base = band_id * band_rows
    place_rows = offsets[0][:, 0, :].reshape(total_subs)
    place_cols = offsets[0][:, 1, :].reshape(total_subs)

    def place(index, padded_tile):
        relative = place_rows[index] - row_base
        intersections = (relative > -side_pix) & (relative < band_rows)
        row_start = jnp.where(intersections, relative + side_pix, 0)
        uv_grid = grid_stack[index] * intersections.astype(jnp.float32)
        starts = (jnp.zeros((), jnp.int32), row_start, place_cols[index])
        current = lax.dynamic_slice(padded_tile, starts, uv_grid.shape)
        return lax.dynamic_update_slice(padded_tile, current + uv_grid, starts)

    padded_tile = jnp.zeros((2, band_rows + 2 * side_pix, tile_side), jnp.float32)
    padded_tile = lax.fori_loop(0, total_subs, place, padded_tile)
    own_rows = padded_tile[:, side_pix : side_pix + band_rows, :]
    return own_rows[None]


def solution(mesh):
    placed = (
        P("facet", None, "band", None, None),
        P(),
        P("facet", None, None, None, None),
        P("facet", None, None, None),
        P("facet", None),
        P(),
    )
    return jax.shard_map(
        body, mesh=mesh, in_specs=placed, out_specs=P("facet", None, "band", None), check_vma=False
    )
```

profile of v0, /device:TPU:0, one launch (start us, length us, event | category | flops | bytes accessed | tf_op | source)
XLA Modules:
  0.0 431.5 jit_solution(16140185295980370585)
XLA Ops:
  8.2 203.8 %while.27 = (s32[]{:T(128)}, f32[4,4,2,1024]{3,2,1,0:T(2,128)}, f32[]{:T(128)}, s32[4]{0:T(128)S(1)}, f32[4,4,2,256]{3,2,1,0:T(2,128)}, /*index=5*/s32[4]{0:T(12...) while((s32[]{:T(128)}, f32[4,4,2,1024]{3,2,1,0:T(2,128)}, ...), condition=%wide.region_2.3_spmd.clone.clone, body=%wide.region_0.2_spmd.clone.clone.sunk | while | flops 149070160 | bytes 10281985 | solution.py:109
  10.8 1.2 dynamic_slice.64
  14.4 7.5 %fusion.182 = (bf16[32,4096]{1,0:T(8,128)(2,1)S(1)}, bf16[32,4096]{1,0:T(8,128)(2,1)S(1)}, bf16[32,4096]{1,0:T(8,128)(2,1)S(1)}, bf16[32,4096]{1,0:T(8,128)(2,1)...) fusion(f32[4096]{0:T(1024)S(1)} %bitcast.209, ...), kind=kLoop, calls=%fused_computation.53.clone.1 | loop fusion | flops 1572864 | bytes 2162816 | tf_op jit(solution)/shard_map/convert.20
  22.0 26.1 %all-reduce.5.cloned.1.call-done = bf16[4,16,2,256]{3,2,1,0:T(2,128)(2,1)} async-done(((bf16[4,16,2,256]{3,2,1,0:T(2,128)(2,1)}), bf16[4,16,2,256]{3,2,1,0:T(2,128)(2,1)}) %all-reduce.5.cloned.1.call-update) | async-done | bytes 65552 | tf_op jit(solution)/shard_map/while/body/eval_jaxpr/psum | solution.py:17
  49.0 8.8 %fusion.181 = (bf16[32,4096]{1,0:T(8,128)(2,1)S(1)}, bf16[32,4096]{1,0:T(8,128)(2,1)S(1)}, bf16[32,4096]{1,0:T(8,128)(2,1)S(1)}, bf16[32,4096]{1,0:T(8,128)(2,1)...) fusion(f32[4096]{0:T(1024)S(1)} %bitcast.215, ...), kind=kLoop, calls=%fused_computation.50.clone.1 | loop fusion | flops 4718592 | bytes 2293888 | tf_op jit(solution)/shard_map/convert.22
  58.3 1.2 fusion.184
  64.1 1.2 dynamic_slice.64
  67.8 7.5 %fusion.182 = (bf16[32,4096]{1,0:T(8,128)(2,1)S(1)}, bf16[32,4096]{1,0:T(8,128)(2,1)S(1)}, bf16[32,4096]{1,0:T(8,128)(2,1)S(1)}, bf16[32,4096]{1,0:T(8,128)(2,1)...) fusion(f32[4096]{0:T(1024)S(1)} %bitcast.209, ...), kind=kLoop, calls=%fused_computation.53.clone.1 | loop fusion | flops 1572864 | bytes 2162816 | tf_op jit(solution)/shard_map/convert.20
  75.4 22.6 %all-reduce.5.cloned.1.call-done = bf16[4,16,2,256]{3,2,1,0:T(2,128)(2,1)} async-done(((bf16[4,16,2,256]{3,2,1,0:T(2,128)(2,1)}), bf16[4,16,2,256]{3,2,1,0:T(2,128)(2,1)}) %all-reduce.5.cloned.1.call-update) | async-done | bytes 65552 | tf_op jit(solution)/shard_map/while/body/eval_jaxpr/psum | solution.py:17
  98.9 8.8 %fusion.181 = (bf16[32,4096]{1,0:T(8,128)(2,1)S(1)}, bf16[32,4096]{1,0:T(8,128)(2,1)S(1)}, bf16[32,4096]{1,0:T(8,128)(2,1)S(1)}, bf16[32,4096]{1,0:T(8,128)(2,1)...) fusion(f32[4096]{0:T(1024)S(1)} %bitcast.215, ...), kind=kLoop, calls=%fused_computation.50.clone.1 | loop fusion | flops 4718592 | bytes 2293888 | tf_op jit(solution)/shard_map/convert.22
  108.1 1.2 fusion.184
  114.0 1.2 dynamic_slice.64
  117.6 7.5 %fusion.182 = (bf16[32,4096]{1,0:T(8,128)(2,1)S(1)}, bf16[32,4096]{1,0:T(8,128)(2,1)S(1)}, bf16[32,4096]{1,0:T(8,128)(2,1)S(1)}, bf16[32,4096]{1,0:T(8,128)(2,1)...) fusion(f32[4096]{0:T(1024)S(1)} %bitcast.209, ...), kind=kLoop, calls=%fused_computation.53.clone.1 | loop fusion | flops 1572864 | bytes 2162816 | tf_op jit(solution)/shard_map/convert.20
  125.2 22.6 %all-reduce.5.cloned.1.call-done = bf16[4,16,2,256]{3,2,1,0:T(2,128)(2,1)} async-done(((bf16[4,16,2,256]{3,2,1,0:T(2,128)(2,1)}), bf16[4,16,2,256]{3,2,1,0:T(2,128)(2,1)}) %all-reduce.5.cloned.1.call-update) | async-done | bytes 65552 | tf_op jit(solution)/shard_map/while/body/eval_jaxpr/psum | solution.py:17
  148.8 8.8 %fusion.181 = (bf16[32,4096]{1,0:T(8,128)(2,1)S(1)}, bf16[32,4096]{1,0:T(8,128)(2,1)S(1)}, bf16[32,4096]{1,0:T(8,128)(2,1)S(1)}, bf16[32,4096]{1,0:T(8,128)(2,1)...) fusion(f32[4096]{0:T(1024)S(1)} %bitcast.215, ...), kind=kLoop, calls=%fused_computation.50.clone.1 | loop fusion | flops 4718592 | bytes 2293888 | tf_op jit(solution)/shard_map/convert.22
  158.0 1.2 fusion.184
  163.9 1.2 dynamic_slice.64
  165.8 1.5 fusion.179
  168.3 7.5 %fusion.182 = (bf16[32,4096]{1,0:T(8,128)(2,1)S(1)}, bf16[32,4096]{1,0:T(8,128)(2,1)S(1)}, bf16[32,4096]{1,0:T(8,128)(2,1)S(1)}, bf16[32,4096]{1,0:T(8,128)(2,1)...) fusion(f32[4096]{0:T(1024)S(1)} %bitcast.209, ...), kind=kLoop, calls=%fused_computation.53.clone.1 | loop fusion | flops 1572864 | bytes 2162816 | tf_op jit(solution)/shard_map/convert.20
  175.9 22.6 %all-reduce.5.cloned.1.call-done = bf16[4,16,2,256]{3,2,1,0:T(2,128)(2,1)} async-done(((bf16[4,16,2,256]{3,2,1,0:T(2,128)(2,1)}), bf16[4,16,2,256]{3,2,1,0:T(2,128)(2,1)}) %all-reduce.5.cloned.1.call-update) | async-done | bytes 65552 | tf_op jit(solution)/shard_map/while/body/eval_jaxpr/psum | solution.py:17
  199.5 8.8 %fusion.181 = (bf16[32,4096]{1,0:T(8,128)(2,1)S(1)}, bf16[32,4096]{1,0:T(8,128)(2,1)S(1)}, bf16[32,4096]{1,0:T(8,128)(2,1)S(1)}, bf16[32,4096]{1,0:T(8,128)(2,1)...) fusion(f32[4096]{0:T(1024)S(1)} %bitcast.215, ...), kind=kLoop, calls=%fused_computation.50.clone.1 | loop fusion | flops 4718592 | bytes 2293888 | tf_op jit(solution)/shard_map/convert.22
  208.7 1.2 fusion.184
  212.0 1.3 slice_reduce_fusion.1
  218.5 72.0 %all-reduce.3.cloned.1.call-done = f32[16,2,32,32]{3,2,0,1:T(8,128)} async-done(((f32[16,2,32,32]{3,2,0,1:T(8,128)}), f32[16,2,32,32]{3,2,0,1:T(8,128)}) %all-reduce.3.cloned.1.call-update) | async-done | bytes 131088 | tf_op jit(solution)/shard_map/psum | solution.py:120
  290.5 3.0 broadcast_in_dim.16
  293.4 126.3 %while.26 = (s32[]{:T(128)}, f32[2,320,2048]{2,1,0:T(8,128)}, s32[16]{0:T(128)S(1)}, s32[]{:T(128)}, s32[16]{0:T(128)S(1)}, /*index=5*/f32[16,2,32,32]{3,2,0,1:T...) while((s32[]{:T(128)}, f32[2,320,2048]{2,1,0:T(8,128)}, ...), condition=%wide.region_5.6_spmd, body=%wide.region_4.5_spmd.sunk | while | flops 4111 | bytes 41268 | solution.py:136
  297.2 1.0 fusion.170
  298.2 3.1 dynamic_update_slice.17
  306.1 3.1 dynamic_update_slice.17
  313.0 1.0 fusion.170
  314.0 3.1 dynamic_update_slice.17
  321.9 3.1 dynamic_update_slice.17
  329.8 3.1 dynamic_update_slice.17
  337.7 3.1 dynamic_update_slice.17
  345.6 3.1 dynamic_update_slice.17
  352.5 1.0 fusion.170
  353.5 3.1 dynamic_update_slice.17
  360.4 1.0 fusion.170
  361.4 3.1 dynamic_update_slice.17
  369.3 3.1 dynamic_update_slice.17
  377.1 3.1 dynamic_update_slice.17
  385.0 3.1 dynamic_update_slice.17
  392.9 3.1 dynamic_update_slice.17
  399.8 1.0 fusion.170
  400.8 3.1 dynamic_update_slice.17
  408.7 3.1 dynamic_update_slice.17
  416.6 3.1 dynamic_update_slice.17
  419.7 4.7 %slice_bitcast_fusion.4 = f32[1,2,256,2048]{3,2,1,0:T(8,128)} fusion(f32[2,320,2048]{2,1,0:T(8,128)} %get-tuple-element.196), kind=kLoop, calls=%fused_computation.142 | loop fusion | bytes 8388608 | tf_op jit(solution)/shard_map/broadcast_in_dim | solution.py:138
  (228 shorter events, 57.7 us)
Async XLA Ops:
  8.2 205.4 %copy-start = (bf16[1,4,4,2,1024]{4,3,2,1,0:T(2,128)(2,1)S(1)}, bf16[1,4,4,2,1024]{4,3,2,1,0:T(2,128)(2,1)}, u32[]{:S(2)}) copy-start(bf16[1,4,4,2,1024]{4,3,2,1,0:T(2,128)(2,1)} %param.12) | copy-start | bytes 196612
  8.2 39.9 %all-reduce.5.cloned.1.call-start = ((), (), s32[]{:S(2)}) async-start(), calls=%async_computation.1 | async-start | bytes 131072 | tf_op jit(solution)/shard_map/while/body/eval_jaxpr/psum | solution.py:17
  61.6 36.4 %all-reduce.5.cloned.1.call-start = ((), (), s32[]{:S(2)}) async-start(), calls=%async_computation.1 | async-start | bytes 131072 | tf_op jit(solution)/shard_map/while/body/eval_jaxpr/psum | solution.py:17
  111.5 36.4 %all-reduce.5.cloned.1.call-start = ((), (), s32[]{:S(2)}) async-start(), calls=%async_computation.1 | async-start | bytes 131072 | tf_op jit(solution)/shard_map/while/body/eval_jaxpr/psum | solution.py:17
  161.3 37.2 %all-reduce.5.cloned.1.call-start = ((), (), s32[]{:S(2)}) async-start(), calls=%async_computation.1 | async-start | bytes 131072 | tf_op jit(solution)/shard_map/while/body/eval_jaxpr/psum | solution.py:17
  212.0 6.3 %copy-start.1 = (s32[1,4,2,4]{3,2,1,0:T(2,128)S(1)}, s32[1,4,2,4]{3,2,1,0:T(2,128)}, u32[]{:S(2)}) copy-start(s32[1,4,2,4]{3,2,1,0:T(2,128)} %param.13) | copy-start | bytes 388
  212.0 78.5 %all-reduce.3.cloned.1.call-start = ((), (), s32[]{:S(2)}) async-start(), calls=%async_computation | async-start | bytes 1048576 | tf_op jit(solution)/shard_map/psum | solution.py:120
Sparse Core Ops, SparseCore 0:
  13.5 34.5 all-reduce.4
  66.9 31.0 all-reduce.4
  116.7 31.0 all-reduce.4
  167.4 31.0 all-reduce.4
Sparse Core Ops, SparseCore 1:
  218.4 72.0 all-reduce.2
where the time goes:
time: 437 us; the launch traced here: 432 us
  waiting for transfers between devices  166 us (38%)
  local copies, waits for them, and re-layouts  94.8 us (22%)
  other arithmetic  91.2 us (21%)
  loops' own time  52.9 us (12%)
  between operations  14.6 us (3%)
  matrix products  11.9 us (3%)
    psum x4, waiting for transfers between devices, spread(): return lax.psum(block, axis)  93.9 us
    psum x1, waiting for transfers between devices, body(): grid_stack = lax.psum(local_grids, 'band')  72 us
    another operation x8, other arithmetic  65.2 us
    dynamic_update_slice x16, local copies, waits for them, and re-layouts, place(): return lax.dynamic_update_slice(padded_tile, current + uv_grid, starts)  49.7 us
    another operation x1, loops' own time, body(): padded_tile = lax.fori_loop(0, total_subs, place, padded_tile)  41.8 us
    add x16, other arithmetic, place(): return lax.dynamic_update_slice(padded_tile, current + uv_grid, starts)  16 us
    another operation x1, loops' own time, body(): lax.scan(advance, jnp.zeros((), jnp.int32), step_order)  11.2 us
    dynamic_slice x16, local copies, waits for them, and re-layouts, place(): starts = (jnp.zeros((), jnp.int32), row_start, place_cols[index])  9.41 us
  transfers between devices with their start and end apart: 5, of which 5 were waited for; matrix products, arithmetic and copies ran while one was open for 8% of the time, Pallas kernels for 0%

commit v1 on v0

v1 whole, which is shorter than its diff:
```python
import functools
import math

import jax
import jax.numpy as jnp
import numpy as np
from jax import lax
from jax.experimental import pallas as pl
from jax.experimental.pallas import tpu as pltpu
from jax.sharding import PartitionSpec as P

NPIX = 32
TILE = 2048
TWO_PI = 2.0 * math.pi
MESH = pl.DeviceIdType.MESH
HIGHEST = lax.Precision.HIGHEST
ROWS = 64


def cmul(a, b):
    return a[0] * b[0] - a[1] * b[1], a[0] * b[1] + a[1] * b[0]


def cheb(two_cos, now, before):
    return two_cos * now[0] - before[0], two_cos * now[1] - before[1]


def pick(mask, a, b):
    return jnp.where(mask, a[0], b[0]), jnp.where(mask, a[1], b[1])


def image_kernel(
    sizes, owner_ref, uv_ref, vis_ref, ate_ref, dft_ref, sel_ref, out_ref,
    pow_ref, left_ref, right_ref, part_ref, got_ref, sum_ref, gain_ref, send_ref, band_ref,
    send_sem, recv_sem, send2_sem, recv2_sem,
):
    facets, bands, steps, subs, chans, width = sizes
    per_band = NPIX // bands
    lanes = per_band * NPIX
    total = facets * bands
    fac, band = lax.axis_index("facet"), lax.axis_index("band")
    me = fac * bands + band

    barrier = pltpu.get_barrier_semaphore()

    def greet(k, carry):
        to = lax.rem(me + k, total)
        pl.semaphore_signal(
            barrier, inc=1, device_id=(to // bands, lax.rem(to, bands)), device_id_type=MESH
        )
        return carry

    lax.fori_loop(1, total, greet, 0)

    step = jnp.int32(0)
    for t in range(steps):
        step = jnp.where(owner_ref[t] == fac, t, step)
    chan = band * chans + lax.broadcasted_iota(jnp.int32, (chans, 1), 0)
    freq = 1.0 + 0.5 * chan.astype(jnp.float32) / (chans * bands)
    for s in range(subs):
        uv = uv_ref[step, s]
        rows = pl.ds(s * chans, chans)
        for axis in range(2):
            angle = (TWO_PI / NPIX) * (uv[axis : axis + 1, :] * freq)
            w1 = (jnp.cos(angle), jnp.sin(angle))
            w2 = cmul(w1, w1)
            w4 = cmul(w2, w2)
            w8 = cmul(w4, w4)
            if axis == 0:
                w16 = cmul(w8, w8)
                kept = (w1, w4, w8, cmul(w4, w8), w16, cmul(w16, w16))
            else:
                kept = (w1, w2, cmul(w1, w2), w4, w8)
            for i, w in enumerate(kept):
                pow_ref[12 * axis + 2 * i, rows, :] = w[0]
                pow_ref[12 * axis + 2 * i + 1, rows, :] = w[1]

    j = lax.broadcasted_iota(jnp.int32, (8, width), 0)
    bit0, bit1, bit2 = (j & 1) == 1, (j & 2) == 2, (j & 4) == 4
    one = (jnp.ones((8, width), jnp.float32), jnp.zeros((8, width), jnp.float32))

    def subgrid(s):
        for c in range(chans):
            row = pl.ds(s * chans + c, 1)

            def power(index):
                return tuple(
                    jnp.broadcast_to(pow_ref[2 * index + part, row, :], (8, width))
                    for part in range(2)
                )

            cols = pl.ds(c * width, width)
            w1, w4, w8, w12, w16, w32 = (power(i) for i in range(6))
            value = vis_ref[0, s, c].astype(jnp.float32)
            vis = (
                jnp.broadcast_to(value[0:1], (8, width)),
                jnp.broadcast_to(value[1:2], (8, width)),
            )
            e = pick(bit1, pick(bit0, w12, w8), pick(bit0, w4, one))
            e = cmul(e, pick(bit2, w16, one))
            upper = cmul(vis, e)
            lower = cmul(upper, (w32[0], -w32[1]))
            two_cos = 2.0 * w1[0]
            seq_u = [upper, cmul(upper, w1)]
            seq_l = [lower, cmul(lower, w1)]
            for i in range(2, 4):
                seq_u.append(cheb(two_cos, seq_u[i - 1], seq_u[i - 2]))
                seq_l.append(cheb(two_cos, seq_l[i - 1], seq_l[i - 2]))
            for i in range(4):
                for part in range(2):
                    left_ref[pl.ds(ROWS * part + 16 * i, 16), cols] = jnp.concatenate(
                        [seq_l[i][part], seq_u[i][part]], axis=0
                    ).astype(jnp.bfloat16)
            r1, r2, r3, r4, r8 = (power(6 + i) for i in range(5))
            e = pick(bit1, pick(bit0, r3, r2), pick(bit0, r1, one))
            m2 = cmul(e, pick(bit2, r4, one))
            m3 = cmul(m2, r8)
            two_cos = 2.0 * r8[0]
            m1 = cheb(two_cos, m2, m3)
            m0 = cheb(two_cos, m1, m2)
            for part in range(2):
                right_ref[pl.ds(NPIX * part, 16), cols] = jnp.concatenate(
                    [m0[part], m1[part]], axis=0
                ).astype(jnp.bfloat16)
                right_ref[pl.ds(NPIX * part + 16, 16), cols] = jnp.concatenate(
                    [m2[part], m3[part]], axis=0
                ).astype(jnp.bfloat16)
        prod = lax.dot_general(
            left_ref[...], right_ref[...], (((1,), (1,)), ((), ())),
            preferred_element_type=jnp.float32,
        )
        re = prod[:ROWS, :NPIX] - prod[ROWS:, NPIX:]
        im = prod[:ROWS, NPIX:] + prod[ROWS:, :NPIX]
        for part, image in enumerate((re, im)):
            for high in range(4 // per_band):
                pieces = [
                    image[16 * (high * per_band + i) : 16 * (high * per_band + i) + 16]
                    for i in range(per_band)
                ]
                part_ref[:, high, 2 * s + part, :] = jnp.concatenate(pieces, axis=1)

    for s in range(subs):
        subgrid(s)

    pl.semaphore_wait(barrier, total - 1)

    groups = 4 // per_band

    def source(to):
        at = (to // bands * (NPIX // facets) + NPIX // 2 // facets) // per_band + lax.rem(to, bands)
        return part_ref.at[at // groups, lax.rem(at, groups)]

    def spread(k, carry):
        to = lax.rem(me + k, total)
        pltpu.make_async_remote_copy(
            src_ref=source(to), dst_ref=got_ref.at[k], send_sem=send_sem, recv_sem=recv_sem,
            device_id=(to // bands, lax.rem(to, bands)), device_id_type=MESH,
        ).start()
        return carry

    lax.fori_loop(1, total, spread, 0)
    got_ref[0] = source(me)[...]

    first = band * lanes // 128
    chunk = pl.ds(pl.multiple_of(first * 128, 128), 128)
    for t in range(steps):
        for s in range(subs):
            gain = ate_ref[0, t, s, :, chunk].astype(jnp.float32)
            if lanes < 128:
                shift = lax.rem(band * lanes, 128)
                gain = sum(
                    jnp.where(shift == at, gain[:, at : at + lanes], 0.0)
                    for at in range(0, 128, lanes)
                )
            gain_ref[pl.ds(8 * t + 2 * s, 2), :] = gain

    def wait_all(buf, count, sem):
        view = buf.at[pl.ds(1, count)]
        pltpu.make_async_copy(view, view, sem).wait()

    wait_all(got_ref, total - 1, recv_sem)
    for g in range(facets):
        acc = got_ref[lax.rem(me - g * bands + total, total)]
        for b in range(1, bands):
            acc = acc + got_ref[lax.rem(me - g * bands - b + 2 * total, total)]
        sum_ref[g] = acc
    image = jnp.concatenate([sum_ref[owner_ref[t]] for t in range(steps)], axis=0)
    gains = gain_ref[...]
    count = 8 * steps
    even = lax.broadcasted_iota(jnp.int32, (count, lanes), 0) % 2 == 0

    def nxt(x):
        return jnp.concatenate([x[1:], x[:1]], axis=0)

    def prev(x):
        return jnp.concatenate([x[-1:], x[:-1]], axis=0)

    straight = image * gains
    crossed = image * jnp.where(even, nxt(gains), prev(gains))
    weighted = jnp.where(even, straight - nxt(straight), crossed + prev(crossed))
    turned = jnp.where(even, nxt(weighted), -prev(weighted))
    both = jnp.concatenate([weighted, turned], axis=1)
    pixel = lax.broadcasted_iota(jnp.int32, both.shape, 1) % lanes // NPIX
    stacked = jnp.concatenate([jnp.where(pixel == i, both, 0.0) for i in range(per_band)], axis=0)
    half = jnp.dot(stacked, dft_ref[...], precision=HIGHEST, preferred_element_type=jnp.float32)
    row_sub = lax.broadcasted_iota(jnp.int32, half.shape, 0) % 8 // 2
    lane_sub = lax.broadcasted_iota(jnp.int32, half.shape, 1) // NPIX
    half = jnp.where(row_sub == lane_sub, half, 0.0)
    half = jnp.dot(sel_ref[...], half, precision=HIGHEST, preferred_element_type=jnp.float32)
    send_ref[...] = half.astype(jnp.bfloat16)

    def share(k, carry):
        pltpu.make_async_remote_copy(
            src_ref=send_ref, dst_ref=band_ref.at[k], send_sem=send2_sem, recv_sem=recv2_sem,
            device_id=(fac, lax.rem(band + k, bands)), device_id_type=MESH,
        ).start()
        return carry

    lax.fori_loop(1, bands, share, 0)
    band_ref[0] = send_ref[...]
    wait_all(band_ref, bands - 1, recv2_sem)
    group = 2 * per_band
    for b in range(bands):
        block = band_ref[lax.rem(band - b + bands, bands)].astype(jnp.float32)
        for t in range(steps):
            out_ref[t, pl.ds(group * b, group), :] = block[group * t : group * t + group]
    wait_all(got_ref, total - 1, send_sem)
    wait_all(band_ref, bands - 1, send2_sem)


def place_kernel(sizes, scale, off_ref, cnt_ref, half_ref, dft_ref, out_ref, grid_ref, tile_ref, sem):
    steps, subs, rows, cols = sizes
    base = lax.axis_index("band") * rows
    tile_ref[:, pl.ds(NPIX, rows), :] = jnp.zeros((2, rows, cols), jnp.float32)
    lane = lax.broadcasted_iota(jnp.int32, (2 * NPIX, 128), 1)

    def one_step(t, carry):
        grid_ref[...] = scale * jnp.dot(
            dft_ref[...], half_ref[t], precision=HIGHEST, preferred_element_type=jnp.float32
        )
        for s in range(subs):
            row = off_ref[0, t, 0, s] - base
            col = off_ref[0, t, 1, s]
            live = (s < cnt_ref[0, t]) & (row > -NPIX) & (row < rows)

            @pl.when(live)
            def _():
                shift = col % 128
                left = pl.multiple_of(col - shift, 128)
                grid = jnp.where(lane // NPIX == s, grid_ref[...], 0.0)
                grid = pltpu.roll(grid, (shift + 128 - NPIX * s) % 128, 1)
                down = (row + NPIX) % 8
                top = pl.multiple_of(row + NPIX - down, 8)
                tail = jnp.zeros((8, 128), jnp.float32)
                parts = [
                    pltpu.roll(
                        jnp.concatenate([grid[NPIX * part : NPIX * part + NPIX], tail], axis=0),
                        down, 0,
                    )
                    for part in range(2)
                ]
                span = lane[: NPIX + 8]
                for part in range(2):
                    spot = (part, pl.ds(top, NPIX + 8), pl.ds(left, 128))
                    tile_ref[spot] += jnp.where(span >= shift, parts[part], 0.0)

                @pl.when(shift > 128 - NPIX)
                def _():
                    right = pl.multiple_of(left + 128, 128)
                    for part in range(2):
                        spot = (part, pl.ds(top, NPIX + 8), pl.ds(right, 128))
                        tile_ref[spot] += jnp.where(span < shift, parts[part], 0.0)

        return carry

    lax.fori_loop(0, steps, one_step, 0)
    copy = pltpu.make_async_copy(tile_ref.at[:, pl.ds(NPIX, rows), :], out_ref.at[0], sem)
    copy.start()
    copy.wait()


def tables(bands, steps, subs):
    per_band = NPIX // bands
    k = np.arange(NPIX)
    angle = 2.0 * np.pi * (k[:, None] * k[None, :] % NPIX) / NPIX
    cos, sin = np.cos(angle), np.sin(angle)
    lanes_dft = np.concatenate(
        [np.tile(cos, (per_band, subs)), np.tile(sin, (per_band, subs))], axis=0
    )
    select = np.zeros((steps, 2, per_band, per_band, steps, subs, 2))
    for t in range(steps):
        for part in range(2):
            for i in range(per_band):
                select[t, part, i, i, t, :, part] = 1.0
    select = select.reshape(steps * 2 * per_band, per_band * steps * subs * 2)
    blocks = np.stack([np.stack([cos, sin]), np.stack([-sin, cos])])
    rows_dft = blocks.reshape(2, 2, NPIX, bands, per_band).transpose(0, 2, 3, 1, 4)
    rows_dft = rows_dft.reshape(2 * NPIX, 2 * NPIX)
    return [np.asarray(x, np.float32) for x in (lanes_dft, select, rows_dft)]


def body(visibilities, uv_coords, aterms, offsets, counts, owner):
    facets, bands = lax.axis_size("facet"), lax.axis_size("band")
    subs, chans, width = visibilities.shape[1], visibilities.shape[2], visibilities.shape[4]
    steps = owner.shape[0]
    per_band = NPIX // bands
    lanes = per_band * NPIX
    total = facets * bands
    lanes_dft, select, rows_dft = tables(bands, steps, subs)
    vmem = pl.BlockSpec(memory_space=pltpu.VMEM)
    smem = pl.BlockSpec(memory_space=pltpu.SMEM)
    f32, bf16 = jnp.float32, jnp.bfloat16
    dma = pltpu.SemaphoreType.DMA(())
    half = pl.pallas_call(
        functools.partial(image_kernel, (facets, bands, steps, subs, chans, width)),
        out_shape=jax.ShapeDtypeStruct((steps, 2 * NPIX, subs * NPIX), f32),
        in_specs=[smem] + [vmem] * 5,
        out_specs=vmem,
        scratch_shapes=[
            pltpu.VMEM((22, subs * chans, width), f32),
            pltpu.VMEM((2 * ROWS, chans * width), bf16),
            pltpu.VMEM((2 * NPIX, chans * width), bf16),
            pltpu.VMEM((16, 4 // per_band, 2 * subs, lanes), f32),
            pltpu.VMEM((total, 2 * subs, lanes), f32),
            pltpu.VMEM((facets, 2 * subs, lanes), f32),
            pltpu.VMEM((8 * steps, lanes), f32),
            pltpu.VMEM((2 * steps * per_band, subs * NPIX), bf16),
            pltpu.VMEM((bands, 2 * steps * per_band, subs * NPIX), bf16),
            dma, dma, dma, dma,
        ],
        compiler_params=pltpu.CompilerParams(
            collective_id=0, has_side_effects=True, vmem_limit_bytes=32 * 1024 * 1024
        ),
    )(owner, uv_coords, visibilities, aterms, lanes_dft, select)
    rows = TILE // bands
    scale = 1.0 / (NPIX * math.sqrt(width * chans * bands))
    return pl.pallas_call(
        functools.partial(place_kernel, (steps, subs, rows, TILE), scale),
        out_shape=jax.ShapeDtypeStruct((1, 2, rows, TILE), f32),
        in_specs=[smem, smem, vmem, vmem],
        out_specs=pl.BlockSpec(memory_space=pl.ANY),
        scratch_shapes=[
            pltpu.VMEM((2 * NPIX, subs * NPIX), f32),
            pltpu.VMEM((2, rows + 2 * NPIX, TILE), f32),
            dma,
        ],
        compiler_params=pltpu.CompilerParams(vmem_limit_bytes=32 * 1024 * 1024),
    )(offsets, counts, half, rows_dft)


def solution(mesh):
    placed = (
        P("facet", None, "band", None, None),
        P(),
        P("facet", None, None, None, None),
        P("facet", None, None, None),
        P("facet", None),
        P(),
    )
    return jax.shard_map(
        body, mesh=mesh, in_specs=placed, out_specs=P("facet", None, "band", None), check_vma=False
    )
```

time: 437 us -> 28.6 us (0.07); the launches traced: 432 us -> 28.2 us
  waiting for transfers between devices: 166 us -> 0 us
  other arithmetic: 91.2 us -> 0 us
  local copies, waits for them, and re-layouts: 94.8 us -> 6.81 us
  loops' own time: 52.9 us -> 0 us
  Pallas kernels: 0 us -> 21.3 us
  between operations: 14.6 us -> 0.03 us
  matrix products: 11.9 us -> 0 us
    psum x5 -> x0, waiting for transfers between devices: 166 us -> none  [the longest x4 93.9 us: spread(): return lax.psum(block, axis)]
    another operation x24 -> x0, other arithmetic: 65.4 us -> none
    another operation x2 -> x0, loops' own time: 52.9 us -> none  [the longest x1 41.8 us: body(): padded_tile = lax.fori_loop(0, total_subs, place, padded_tile)]
    dynamic_update_slice x16 -> x0, local copies, waits for them, and re-layouts: 49.7 us -> none  [place(): return lax.dynamic_update_slice(padded_tile, current + uv_grid, starts)]
    dynamic_slice x40 -> x0, local copies, waits for them, and re-layouts: 26 us -> none  [the longest x16 9.41 us: place(): starts = (jnp.zeros((), jnp.int32), row_start, place_cols[index])]
    pallas_call x0 -> x2, Pallas kernels: none -> 21.3 us  [the longest x1 17.6 us: body(): pl.pallas_call(functools.partial(image_kernel, (facets, bands, steps, sub...]
    add x20 -> x0, other arithmetic: 16.1 us -> none  [the longest x16 16 us: place(): return lax.dynamic_update_slice(padded_tile, current + uv_grid, starts)]
    dot_general x24 -> x0, matrix products: 11.9 us -> none  [the longest x16 8.38 us: subgrid_image(): lax.dot_general(left_ops, right_ops, (((1,), (1,)), ((), ())), preferred_...]
  transfers between devices with their start and end apart: 5 -> 0, of which waited for: 5 -> 0; matrix products, arithmetic and copies ran while one was open for 8% -> 0% of each run, Pallas kernels for 0% -> 0%
where the time goes in v1:
time: 28.6 us; the launch traced here: 28.2 us
  Pallas kernels  21.3 us (74%)
  local copies, waits for them, and re-layouts  6.81 us (24%)
    pallas_call x1, Pallas kernels, body(): pl.pallas_call(functools.partial(image_kernel, (facets, bands, steps, sub...  17.6 us
    unnamed x18, local copies, waits for them, and re-layouts  6.81 us
    pallas_call x1, Pallas kernels, body(): pl.pallas_call(functools.partial(place_kernel, (steps, subs, rows, TILE),...  3.77 us

profile of v1, /device:TPU:0, one launch (start us, length us, event | category | flops | bytes accessed | tf_op | source)
XLA Modules:
  0.0 28.2 jit_solution(3907531154599101258)
XLA Ops:
  0.0 0.0 copy-start
  0.0 0.9 %copy-done = f32[256,128]{1,0:T(8,128)S(1)} copy-done((f32[256,128]{1,0:T(8,128)S(1)}, f32[256,128]{1,0:T(8,128)}, u32[]{:S(2)}) %copy-start) | copy-done | bytes 131096
  0.9 0.0 copy-start.1
  0.9 0.8 %copy-done.1 = bf16[1,4,16,2,256]{4,3,2,1,0:T(2,128)(2,1)S(1)} copy-done((bf16[1,4,16,2,256]{4,3,2,1,0:T(2,128)(2,1)S(1)}, bf16[1,4,16,2,256]{4,3,2,1,0:T(2,128)(2,1)}, u32[]{:S(2)}) %copy-start.1) | copy-done | bytes 65560
  1.7 0.0 copy-start.2
  1.7 0.8 %copy-done.2 = bf16[1,4,4,2,1024]{4,3,2,1,0:T(2,128)(2,1)S(1)} copy-done((bf16[1,4,4,2,1024]{4,3,2,1,0:T(2,128)(2,1)S(1)}, bf16[1,4,4,2,1024]{4,3,2,1,0:T(2,128)(2,1)}, u32[]{:S(2)}) %copy-start.2) | copy-done | bytes 65560
  2.6 0.0 copy-start.4
  2.6 0.8 %copy-done.4 = f32[4,4,2,256]{3,2,1,0:T(2,128)S(1)} copy-done((f32[4,4,2,256]{3,2,1,0:T(2,128)S(1)}, f32[4,4,2,256]{3,2,1,0:T(2,128)}, u32[]{:S(2)}) %copy-start.4) | copy-done | bytes 32792
  3.3 0.0 copy-start.5
  3.3 0.7 %copy-done.5 = f32[32,128]{1,0:T(8,128)S(1)} copy-done((f32[32,128]{1,0:T(8,128)S(1)}, f32[32,128]{1,0:T(8,128)}, u32[]{:S(2)}) %copy-start.5) | copy-done | bytes 16408
  4.1 0.0 copy-start.7
  4.1 0.7 %copy-done.7 = s32[4]{0:T(128)S(1)} copy-done((s32[4]{0:T(128)S(1)}, s32[4]{0:T(128)}, u32[]{:S(2)}) %copy-start.7) | copy-done | bytes 40
  4.7 17.6 %shard_map.91.half_ref = f32[4,64,128]{2,1,0:T(8,128)S(1)} custom-call(s32[4]{0:T(128)S(1)} %copy-done.7, f32[4,4,2,256]{3,2,1,0:T(2,128)S(1)} %copy-done.4, bf16[1,4,16,2,256]{4,3,2,1,0:T(2,128)(2,1)S(1)} %copy-done.1, bf16[1,4,4,2,1024]{4,3,2,1,0:T(2,128)(2,1)S(1)} %copy-done.2, f32[256,128]{1,0:T(8,128)S(1)} %copy-done, f32[32,128]{1,0:T(8,128)S(1)} %copy-done.5), custom_call_target="tpu_custom_call" | custom-call | tf_op jit(solution)/shard_map/pallas_call | solution.py:314
  22.3 0.0 copy-start.3
  22.3 0.7 %copy-done.3 = f32[64,64]{1,0:T(8,128)S(1)} copy-done((f32[64,64]{1,0:T(8,128)S(1)}, f32[64,64]{1,0:T(8,128)}, u32[]{:S(2)}) %copy-start.3) | copy-done | bytes 16408
  23.0 0.0 copy-start.6
  23.0 0.7 %copy-done.6 = s32[1,4,2,4]{3,2,1,0:T(2,128)S(1)} copy-done((s32[1,4,2,4]{3,2,1,0:T(2,128)S(1)}, s32[1,4,2,4]{3,2,1,0:T(2,128)}, u32[]{:S(2)}) %copy-start.6) | copy-done | bytes 152
  23.7 0.0 copy-start.8
  23.7 0.7 %copy-done.8 = s32[1,4]{1,0:T(1,128)S(1)} copy-done((s32[1,4]{1,0:T(1,128)S(1)}, s32[1,4]{1,0:T(1,128)}, u32[]{:S(2)}) %copy-start.8) | copy-done | bytes 40
  24.4 3.8 %shard_map.92 = f32[1,2,256,2048]{3,2,1,0:T(8,128)} custom-call(s32[1,4,2,4]{3,2,1,0:T(2,128)S(1)} %copy-done.6, s32[1,4]{1,0:T(1,128)S(1)} %copy-done.8, f32[4,64,128]{2,1,0:T(8,128)S(1)} %shard_map.91.half_ref, f32[64,64]{1,0:T(8,128)S(1)} %copy-done.3), custom_call_target="tpu_custom_call" | custom-call | tf_op jit(solution)/shard_map/pallas_call | solution.py:337
Async XLA Ops:
  0.0 0.9 %copy-start = (f32[256,128]{1,0:T(8,128)S(1)}, f32[256,128]{1,0:T(8,128)}, u32[]{:S(2)}) copy-start(f32[256,128]{1,0:T(8,128)} %constant.6.clone.dft_ref) | copy-start | bytes 393220
  0.9 0.8 %copy-start.1 = (bf16[1,4,16,2,256]{4,3,2,1,0:T(2,128)(2,1)S(1)}, bf16[1,4,16,2,256]{4,3,2,1,0:T(2,128)(2,1)}, u32[]{:S(2)}) copy-start(bf16[1,4,16,2,256]{4,3,2,1,0:T(2,128)(2,1)} %vis_ref.1) | copy-start | bytes 196612
  1.7 0.8 %copy-start.2 = (bf16[1,4,4,2,1024]{4,3,2,1,0:T(2,128)(2,1)S(1)}, bf16[1,4,4,2,1024]{4,3,2,1,0:T(2,128)(2,1)}, u32[]{:S(2)}) copy-start(bf16[1,4,4,2,1024]{4,3,2,1,0:T(2,128)(2,1)} %ate_ref.1) | copy-start | bytes 196612
  2.6 0.8 %copy-start.4 = (f32[4,4,2,256]{3,2,1,0:T(2,128)S(1)}, f32[4,4,2,256]{3,2,1,0:T(2,128)}, u32[]{:S(2)}) copy-start(f32[4,4,2,256]{3,2,1,0:T(2,128)} %uv_ref.1) | copy-start | bytes 98308
  3.3 0.7 %copy-start.5 = (f32[32,128]{1,0:T(8,128)S(1)}, f32[32,128]{1,0:T(8,128)}, u32[]{:S(2)}) copy-start(f32[32,128]{1,0:T(8,128)} %constant.7.clone.sel_ref) | copy-start | bytes 49156
  4.1 0.7 %copy-start.7 = (s32[4]{0:T(128)S(1)}, s32[4]{0:T(128)}, u32[]{:S(2)}) copy-start(s32[4]{0:T(128)} %owner_ref.1) | copy-start | bytes 52
  22.3 0.8 %copy-start.3 = (f32[64,64]{1,0:T(8,128)S(1)}, f32[64,64]{1,0:T(8,128)}, u32[]{:S(2)}) copy-start(f32[64,64]{1,0:T(8,128)} %constant.8.clone.dft_ref) | copy-start | bytes 49156
  23.0 0.7 %copy-start.6 = (s32[1,4,2,4]{3,2,1,0:T(2,128)S(1)}, s32[1,4,2,4]{3,2,1,0:T(2,128)}, u32[]{:S(2)}) copy-start(s32[1,4,2,4]{3,2,1,0:T(2,128)} %off_ref.1) | copy-start | bytes 388
  23.7 0.7 %copy-start.8 = (s32[1,4]{1,0:T(1,128)S(1)}, s32[1,4]{1,0:T(1,128)}, u32[]{:S(2)}) copy-start(s32[1,4]{1,0:T(1,128)} %cnt_ref.1) | copy-start | bytes 52

commit v2 on v1

--- a/solution.py
+++ b/solution.py
@@ -14,6 +14,7 @@
 TWO_PI = 2.0 * math.pi
 MESH = pl.DeviceIdType.MESH
 HIGHEST = lax.Precision.HIGHEST
+VMEM_LIMIT = 60 * 1024 * 1024
 ROWS = 64
 
 
@@ -30,7 +31,8 @@
 
 
 def image_kernel(
-    sizes, owner_ref, uv_ref, vis_ref, ate_ref, dft_ref, sel_ref, out_ref,
+    sizes, owner_hbm, uv_hbm, vis_hbm, ate_hbm, dft_hbm, sel_hbm, out_ref,
+    owner_ref, uv_ref, vis_ref, ate_ref, dft_ref, sel_ref, load_sem,
     pow_ref, left_ref, right_ref, part_ref, got_ref, sum_ref, gain_ref, send_ref, band_ref,
     send_sem, recv_sem, send2_sem, recv2_sem,
 ):
@@ -41,6 +43,17 @@
     fac, band = lax.axis_index("facet"), lax.axis_index("band")
     me = fac * bands + band
 
+    first = band * lanes // 128
+    chunk = pl.ds(pl.multiple_of(first * 128, 128), 128)
+    loads = [
+        pltpu.make_async_copy(src, dst, load_sem.at[i])
+        for i, (src, dst) in enumerate((
+            (owner_hbm, owner_ref), (uv_hbm, uv_ref), (vis_hbm.at[0], vis_ref),
+            (ate_hbm.at[0, :, :, :, chunk], ate_ref), (dft_hbm, dft_ref), (sel_hbm, sel_ref),
+        ))
+    ]
+    for load in loads:
+        load.start()
     barrier = pltpu.get_barrier_semaphore()
 
     def greet(k, carry):
@@ -52,6 +65,8 @@
 
     lax.fori_loop(1, total, greet, 0)
 
+    for load in loads[:3]:
+        load.wait()
     step = jnp.int32(0)
     for t in range(steps):
         step = jnp.where(owner_ref[t] == fac, t, step)
@@ -91,7 +106,7 @@
 
             cols = pl.ds(c * width, width)
             w1, w4, w8, w12, w16, w32 = (power(i) for i in range(6))
-            value = vis_ref[0, s, c].astype(jnp.float32)
+            value = vis_ref[s, c].astype(jnp.float32)
             vis = (
                 jnp.broadcast_to(value[0:1], (8, width)),
                 jnp.broadcast_to(value[1:2], (8, width)),
@@ -161,11 +176,11 @@
     lax.fori_loop(1, total, spread, 0)
     got_ref[0] = source(me)[...]
 
-    first = band * lanes // 128
-    chunk = pl.ds(pl.multiple_of(first * 128, 128), 128)
+    for load in loads[3:]:
+        load.wait()
     for t in range(steps):
         for s in range(subs):
-            gain = ate_ref[0, t, s, :, chunk].astype(jnp.float32)
+            gain = ate_ref[t, s].astype(jnp.float32)
             if lanes < 128:
                 shift = lax.rem(band * lanes, 128)
                 gain = sum(
@@ -228,11 +243,24 @@
     wait_all(band_ref, bands - 1, send2_sem)
 
 
-def place_kernel(sizes, scale, off_ref, cnt_ref, half_ref, dft_ref, out_ref, grid_ref, tile_ref, sem):
+def place_kernel(
+    sizes, scale, off_hbm, cnt_hbm, half_hbm, dft_hbm, out_ref,
+    off_ref, cnt_ref, half_ref, dft_ref, grid_ref, tile_ref, load_sem, sem,
+):
     steps, subs, rows, cols = sizes
+    loads = [
+        pltpu.make_async_copy(src, dst, load_sem.at[i])
+        for i, (src, dst) in enumerate((
+            (off_hbm, off_ref), (cnt_hbm, cnt_ref), (half_hbm, half_ref), (dft_hbm, dft_ref),
+        ))
+    ]
+    for load in loads:
+        load.start()
     base = lax.axis_index("band") * rows
     tile_ref[:, pl.ds(NPIX, rows), :] = jnp.zeros((2, rows, cols), jnp.float32)
     lane = lax.broadcasted_iota(jnp.int32, (2 * NPIX, 128), 1)
+    for load in loads:
+        load.wait()
 
     def one_step(t, carry):
         grid_ref[...] = scale * jnp.dot(
@@ -308,15 +336,22 @@
     total = facets * bands
     lanes_dft, select, rows_dft = tables(bands, steps, subs)
     vmem = pl.BlockSpec(memory_space=pltpu.VMEM)
-    smem = pl.BlockSpec(memory_space=pltpu.SMEM)
+    hbm = pl.BlockSpec(memory_space=pltpu.HBM)
     f32, bf16 = jnp.float32, jnp.bfloat16
     dma = pltpu.SemaphoreType.DMA(())
     half = pl.pallas_call(
         functools.partial(image_kernel, (facets, bands, steps, subs, chans, width)),
         out_shape=jax.ShapeDtypeStruct((steps, 2 * NPIX, subs * NPIX), f32),
-        in_specs=[smem] + [vmem] * 5,
+        in_specs=[hbm] * 6,
         out_specs=vmem,
         scratch_shapes=[
+            pltpu.SMEM(owner.shape, jnp.int32),
+            pltpu.VMEM(uv_coords.shape, f32),
+            pltpu.VMEM(visibilities.shape[1:], bf16),
+            pltpu.VMEM((steps, subs, 2, 128), bf16),
+            pltpu.VMEM(lanes_dft.shape, f32),
+            pltpu.VMEM(select.shape, f32),
+            pltpu.SemaphoreType.DMA((6,)),
             pltpu.VMEM((22, subs * chans, width), f32),
             pltpu.VMEM((2 * ROWS, chans * width), bf16),
             pltpu.VMEM((2 * NPIX, chans * width), bf16),
@@ -329,7 +364,7 @@
             dma, dma, dma, dma,
         ],
         compiler_params=pltpu.CompilerParams(
-            collective_id=0, has_side_effects=True, vmem_limit_bytes=32 * 1024 * 1024
+            collective_id=0, has_side_effects=True, vmem_limit_bytes=VMEM_LIMIT
         ),
     )(owner, uv_coords, visibilities, aterms, lanes_dft, select)
     rows = TILE // bands
@@ -337,14 +372,19 @@
     return pl.pallas_call(
         functools.partial(place_kernel, (steps, subs, rows, TILE), scale),
         out_shape=jax.ShapeDtypeStruct((1, 2, rows, TILE), f32),
-        in_specs=[smem, smem, vmem, vmem],
+        in_specs=[hbm] * 4,
         out_specs=pl.BlockSpec(memory_space=pl.ANY),
         scratch_shapes=[
+            pltpu.SMEM(offsets.shape, jnp.int32),
+            pltpu.SMEM(counts.shape, jnp.int32),
+            pltpu.VMEM(half.shape, f32),
+            pltpu.VMEM(rows_dft.shape, f32),
             pltpu.VMEM((2 * NPIX, subs * NPIX), f32),
             pltpu.VMEM((2, rows + 2 * NPIX, TILE), f32),
+            pltpu.SemaphoreType.DMA((4,)),
             dma,
         ],
-        compiler_params=pltpu.CompilerParams(vmem_limit_bytes=32 * 1024 * 1024),
+        compiler_params=pltpu.CompilerParams(vmem_limit_bytes=VMEM_LIMIT),
     )(offsets, counts, half, rows_dft)
 
 

time: 28.6 us -> 21.7 us (0.76)
  local copies, waits for them, and re-layouts: 6.81 us -> 0 us
    unnamed x18 -> x0, local copies, waits for them, and re-layouts: 6.81 us -> none
where the time goes in v2:
time: 21.7 us; the launch traced here: 21.5 us
  Pallas kernels  21.5 us (99%)
    pallas_call x1, Pallas kernels, body(): pl.pallas_call(functools.partial(image_kernel, (facets, bands, steps, sub...  17.6 us
    pallas_call x1, Pallas kernels, body(): pl.pallas_call(functools.partial(place_kernel, (steps, subs, rows, TILE),...  3.85 us

profile of v2, /device:TPU:0, one launch (start us, length us, event | category | flops | bytes accessed | tf_op | source)
XLA Modules:
  0.0 21.5 jit_solution(812300716503121099)
XLA Ops:
  0.0 17.6 %shard_map.91.half_hbm = f32[4,64,128]{2,1,0:T(8,128)} custom-call(s32[4]{0:T(128)} %owner_hbm.1, f32[4,4,2,256]{3,2,1,0:T(2,128)} %uv_hbm.1, bf16[1,4,16,2,256]{4,3,2,1,0:T(2,128)(2,1)} %vis_hbm.1, bf16[1,4,4,2,1024]{4,3,2,1,0:T(2,128)(2,1)} %ate_hbm.1, f32[256,128]{1,0:T(8,128)} %constant.6.clone.dft_hbm, f32[32,128]{1,0:T(8,128)} %constant.7.clone.sel_hbm), custom_call_target="tpu_custom_call" | custom-call | tf_op jit(solution)/shard_map/pallas_call | solution.py:342
  17.6 3.9 %shard_map.92 = f32[1,2,256,2048]{3,2,1,0:T(8,128)} custom-call(s32[1,4,2,4]{3,2,1,0:T(2,128)} %off_hbm.1, s32[1,4]{1,0:T(1,128)} %cnt_hbm.1, f32[4,64,128]{2,1,0:T(8,128)} %shard_map.91.half_hbm, f32[64,64]{1,0:T(8,128)} %constant.8.clone.dft_hbm), custom_call_target="tpu_custom_call" | custom-call | tf_op jit(solution)/shard_map/pallas_call | solution.py:372

commit v3 on v2

--- a/solution.py
+++ b/solution.py
@@ -33,15 +33,20 @@
 def image_kernel(
     sizes, owner_hbm, uv_hbm, vis_hbm, ate_hbm, dft_hbm, sel_hbm, out_ref,
     owner_ref, uv_ref, vis_ref, ate_ref, dft_ref, sel_ref, load_sem,
-    pow_ref, left_ref, right_ref, part_ref, got_ref, sum_ref, gain_ref, send_ref, band_ref,
-    send_sem, recv_sem, send2_sem, recv2_sem,
+    pow_ref, left_ref, right_ref, part_ref, cast_ref, got_ref, sum_ref, fac_ref, gain_ref,
+    send_ref, band_ref, send_sem, recv_sem, send2_sem, recv2_sem, send3_sem, recv3_sem,
 ):
     facets, bands, steps, subs, chans, width = sizes
     per_band = NPIX // bands
     lanes = per_band * NPIX
-    total = facets * bands
+    groups, stride = 4 // per_band, bands // facets
     fac, band = lax.axis_index("facet"), lax.axis_index("band")
-    me = fac * bands + band
+
+    def in_band(k):
+        return fac, lax.rem(band + k, bands)
+
+    def in_facet(k):
+        return lax.rem(fac + k, facets), band
 
     first = band * lanes // 128
     chunk = pl.ds(pl.multiple_of(first * 128, 128), 128)
@@ -56,14 +61,10 @@
         load.start()
     barrier = pltpu.get_barrier_semaphore()
 
-    def greet(k, carry):
-        to = lax.rem(me + k, total)
-        pl.semaphore_signal(
-            barrier, inc=1, device_id=(to // bands, lax.rem(to, bands)), device_id_type=MESH
-        )
-        return carry
-
-    lax.fori_loop(1, total, greet, 0)
+    for k in range(1, facets):
+        pl.semaphore_signal(barrier, inc=1, device_id=in_facet(k), device_id_type=MESH)
+    for k in range(1, bands):
+        pl.semaphore_signal(barrier, inc=1, device_id=in_band(k), device_id_type=MESH)
 
     for load in loads[:3]:
         load.wait()
@@ -83,7 +84,7 @@
             w8 = cmul(w4, w4)
             if axis == 0:
                 w16 = cmul(w8, w8)
-                kept = (w1, w4, w8, cmul(w4, w8), w16, cmul(w16, w16))
+                kept = (w1, w4, w8, w16, cmul(w8, w16), cmul(w16, w16))
             else:
                 kept = (w1, w2, cmul(w1, w2), w4, w8)
             for i, w in enumerate(kept):
@@ -105,16 +106,16 @@
                 )
 
             cols = pl.ds(c * width, width)
-            w1, w4, w8, w12, w16, w32 = (power(i) for i in range(6))
+            w1, w4, w8, w16, w24, w32 = (power(i) for i in range(6))
             value = vis_ref[s, c].astype(jnp.float32)
             vis = (
                 jnp.broadcast_to(value[0:1], (8, width)),
                 jnp.broadcast_to(value[1:2], (8, width)),
             )
-            e = pick(bit1, pick(bit0, w12, w8), pick(bit0, w4, one))
-            e = cmul(e, pick(bit2, w16, one))
-            upper = cmul(vis, e)
-            lower = cmul(upper, (w32[0], -w32[1]))
+            e = pick(bit1, pick(bit0, w24, w16), pick(bit0, w8, one))
+            e = cmul(e, pick(bit2, one, (w32[0], -w32[1])))
+            lower = cmul(vis, e)
+            upper = cmul(lower, w4)
             two_cos = 2.0 * w1[0]
             seq_u = [upper, cmul(upper, w1)]
             seq_l = [lower, cmul(lower, w1)]
@@ -148,33 +149,38 @@
         im = prod[:ROWS, NPIX:] + prod[ROWS:, :NPIX]
         for part, image in enumerate((re, im)):
             for high in range(4 // per_band):
-                pieces = [
-                    image[16 * (high * per_band + i) : 16 * (high * per_band + i) + 16]
-                    for i in range(per_band)
-                ]
-                part_ref[:, high, 2 * s + part, :] = jnp.concatenate(pieces, axis=1)
+                for odd in range(2):
+                    pieces = []
+                    for i in range(per_band):
+                        at = 16 * (high * per_band + i) + 8 * odd
+                        pieces.append(image[at : at + 8])
+                    piece = jnp.concatenate(pieces, axis=1)
+                    start, hop = odd * groups + high, 2 * groups // stride
+                    for j in range(8):
+                        part_ref[start % stride, start // stride + hop * j, 2 * s + part, :] = (
+                            piece[j]
+                        )
 
     for s in range(subs):
         subgrid(s)
 
-    pl.semaphore_wait(barrier, total - 1)
-
-    groups = 4 // per_band
-
-    def source(to):
-        at = (to // bands * (NPIX // facets) + NPIX // 2 // facets) // per_band + lax.rem(to, bands)
-        return part_ref.at[at // groups, lax.rem(at, groups)]
-
-    def spread(k, carry):
-        to = lax.rem(me + k, total)
+    for b in range(bands):
+        at = stride // 2 + b
+        block = part_ref[at % stride, pl.ds(at // stride, facets)]
+        cast_ref[b] = block.reshape(facets * 2 * subs, lanes).astype(jnp.bfloat16)
+
+    pl.semaphore_wait(barrier, facets + bands - 2)
+
+    def send(src, dst, sems, to):
         pltpu.make_async_remote_copy(
-            src_ref=source(to), dst_ref=got_ref.at[k], send_sem=send_sem, recv_sem=recv_sem,
-            device_id=(to // bands, lax.rem(to, bands)), device_id_type=MESH,
+            src_ref=src, dst_ref=dst, send_sem=sems[0], recv_sem=sems[1],
+            device_id=to, device_id_type=MESH,
         ).start()
-        return carry
-
-    lax.fori_loop(1, total, spread, 0)
-    got_ref[0] = source(me)[...]
+
+    for k in range(1, bands):
+        to = in_band(k)
+        send(cast_ref.at[to[1]], got_ref.at[k], (send_sem, recv_sem), to)
+    got_ref[0] = cast_ref[band]
 
     for load in loads[3:]:
         load.wait()
@@ -193,13 +199,19 @@
         view = buf.at[pl.ds(1, count)]
         pltpu.make_async_copy(view, view, sem).wait()
 
-    wait_all(got_ref, total - 1, recv_sem)
-    for g in range(facets):
-        acc = got_ref[lax.rem(me - g * bands + total, total)]
-        for b in range(1, bands):
-            acc = acc + got_ref[lax.rem(me - g * bands - b + 2 * total, total)]
-        sum_ref[g] = acc
-    image = jnp.concatenate([sum_ref[owner_ref[t]] for t in range(steps)], axis=0)
+    wait_all(got_ref, bands - 1, recv_sem)
+    acc = got_ref[0].astype(jnp.float32)
+    for k in range(1, bands):
+        acc = acc + got_ref[k].astype(jnp.float32)
+    sum_ref[...] = acc.reshape(sum_ref.shape)
+    for k in range(1, facets):
+        to = in_facet(k)
+        send(sum_ref.at[to[0]], fac_ref.at[k], (send2_sem, recv2_sem), to)
+    fac_ref[0] = sum_ref[fac]
+    wait_all(fac_ref, facets - 1, recv2_sem)
+    image = jnp.concatenate(
+        [fac_ref[lax.rem(fac + facets - owner_ref[t], facets)] for t in range(steps)], axis=0
+    )
     gains = gain_ref[...]
     count = 8 * steps
     even = lax.broadcasted_iota(jnp.int32, (count, lanes), 0) % 2 == 0
@@ -224,23 +236,18 @@
     half = jnp.dot(sel_ref[...], half, precision=HIGHEST, preferred_element_type=jnp.float32)
     send_ref[...] = half.astype(jnp.bfloat16)
 
-    def share(k, carry):
-        pltpu.make_async_remote_copy(
-            src_ref=send_ref, dst_ref=band_ref.at[k], send_sem=send2_sem, recv_sem=recv2_sem,
-            device_id=(fac, lax.rem(band + k, bands)), device_id_type=MESH,
-        ).start()
-        return carry
-
-    lax.fori_loop(1, bands, share, 0)
+    for k in range(1, bands):
+        send(send_ref, band_ref.at[k], (send3_sem, recv3_sem), in_band(k))
     band_ref[0] = send_ref[...]
-    wait_all(band_ref, bands - 1, recv2_sem)
+    wait_all(band_ref, bands - 1, recv3_sem)
     group = 2 * per_band
     for b in range(bands):
         block = band_ref[lax.rem(band - b + bands, bands)].astype(jnp.float32)
         for t in range(steps):
             out_ref[t, pl.ds(group * b, group), :] = block[group * t : group * t + group]
-    wait_all(got_ref, total - 1, send_sem)
-    wait_all(band_ref, bands - 1, send2_sem)
+    wait_all(got_ref, bands - 1, send_sem)
+    wait_all(fac_ref, facets - 1, send2_sem)
+    wait_all(band_ref, bands - 1, send3_sem)
 
 
 def place_kernel(
@@ -332,8 +339,7 @@
     subs, chans, width = visibilities.shape[1], visibilities.shape[2], visibilities.shape[4]
     steps = owner.shape[0]
     per_band = NPIX // bands
-    lanes = per_band * NPIX
-    total = facets * bands
+    lanes, stride = per_band * NPIX, bands // facets
     lanes_dft, select, rows_dft = tables(bands, steps, subs)
     vmem = pl.BlockSpec(memory_space=pltpu.VMEM)
     hbm = pl.BlockSpec(memory_space=pltpu.HBM)
@@ -355,13 +361,15 @@
             pltpu.VMEM((22, subs * chans, width), f32),
             pltpu.VMEM((2 * ROWS, chans * width), bf16),
             pltpu.VMEM((2 * NPIX, chans * width), bf16),
-            pltpu.VMEM((16, 4 // per_band, 2 * subs, lanes), f32),
-            pltpu.VMEM((total, 2 * subs, lanes), f32),
+            pltpu.VMEM((stride, ROWS // per_band // stride, 2 * subs, lanes), f32),
+            pltpu.VMEM((bands, facets * 2 * subs, lanes), bf16),
+            pltpu.VMEM((bands, facets * 2 * subs, lanes), bf16),
+            pltpu.VMEM((facets, 2 * subs, lanes), f32),
             pltpu.VMEM((facets, 2 * subs, lanes), f32),
             pltpu.VMEM((8 * steps, lanes), f32),
             pltpu.VMEM((2 * steps * per_band, subs * NPIX), bf16),
             pltpu.VMEM((bands, 2 * steps * per_band, subs * NPIX), bf16),
-            dma, dma, dma, dma,
+            dma, dma, dma, dma, dma, dma,
         ],
         compiler_params=pltpu.CompilerParams(
             collective_id=0, has_side_effects=True, vmem_limit_bytes=VMEM_LIMIT

time: 21.7 us -> 22.8 us (1.051)
  Pallas kernels: 21.5 us -> 22.6 us
    pallas_call x1, Pallas kernels: 17.6 us -> 18.8 us  [body(): pl.pallas_call(functools.partial(image_kernel, (facets, bands, steps, sub...]
where the time goes in v3:
time: 22.8 us; the launch traced here: 22.6 us
  Pallas kernels  22.6 us (99%)
    pallas_call x1, Pallas kernels, body(): pl.pallas_call(functools.partial(image_kernel, (facets, bands, steps, sub...  18.8 us
    pallas_call x1, Pallas kernels, body(): pl.pallas_call(functools.partial(place_kernel, (steps, subs, rows, TILE),...  3.77 us

profile of v3, /device:TPU:0, one launch (start us, length us, event | category | flops | bytes accessed | tf_op | source)
XLA Modules:
  0.0 22.6 jit_solution(787763764758914921)
XLA Ops:
  0.0 18.8 %shard_map.91.half_hbm = f32[4,64,128]{2,1,0:T(8,128)} custom-call(s32[4]{0:T(128)} %owner_hbm.1, f32[4,4,2,256]{3,2,1,0:T(2,128)} %uv_hbm.1, bf16[1,4,16,2,256]{4,3,2,1,0:T(2,128)(2,1)} %vis_hbm.1, bf16[1,4,4,2,1024]{4,3,2,1,0:T(2,128)(2,1)} %ate_hbm.1, f32[256,128]{1,0:T(8,128)} %constant.6.clone.dft_hbm, f32[32,128]{1,0:T(8,128)} %constant.7.clone.sel_hbm), custom_call_target="tpu_custom_call" | custom-call | tf_op jit(solution)/shard_map/pallas_call | solution.py:348
  18.8 3.8 %shard_map.92 = f32[1,2,256,2048]{3,2,1,0:T(8,128)} custom-call(s32[1,4,2,4]{3,2,1,0:T(2,128)} %off_hbm.1, s32[1,4]{1,0:T(1,128)} %cnt_hbm.1, f32[4,64,128]{2,1,0:T(8,128)} %shard_map.91.half_hbm, f32[64,64]{1,0:T(8,128)} %constant.8.clone.dft_hbm), custom_call_target="tpu_custom_call" | custom-call | tf_op jit(solution)/shard_map/pallas_call | solution.py:380

commit v4 on v2

--- a/solution.py
+++ b/solution.py
@@ -221,7 +221,10 @@
     row_sub = lax.broadcasted_iota(jnp.int32, half.shape, 0) % 8 // 2
     lane_sub = lax.broadcasted_iota(jnp.int32, half.shape, 1) // NPIX
     half = jnp.where(row_sub == lane_sub, half, 0.0)
-    half = jnp.dot(sel_ref[...], half, precision=HIGHEST, preferred_element_type=jnp.float32)
+    half = jnp.dot(
+        sel_ref[...].astype(jnp.bfloat16), half.astype(jnp.bfloat16),
+        preferred_element_type=jnp.float32,
+    )
     send_ref[...] = half.astype(jnp.bfloat16)
 
     def share(k, carry):
@@ -257,25 +260,48 @@
     for load in loads:
         load.start()
     base = lax.axis_index("band") * rows
-    tile_ref[:, pl.ds(NPIX, rows), :] = jnp.zeros((2, rows, cols), jnp.float32)
+    split = rows // 2
+    cuts = (NPIX, min(split + 2 * NPIX, rows + NPIX), rows + NPIX)
+
+    def clear(first, last):
+        if last > first:
+            tile_ref[:, pl.ds(first, last - first), :] = jnp.zeros(
+                (2, last - first, cols), jnp.float32
+            )
+
+    def write(at):
+        return pltpu.make_async_copy(
+            tile_ref.at[:, pl.ds(NPIX + at * split, split), :],
+            out_ref.at[0, :, pl.ds(at * split, split), :], sem.at[at],
+        )
+
+    clear(cuts[0], cuts[1])
     lane = lax.broadcasted_iota(jnp.int32, (2 * NPIX, 128), 1)
     for load in loads:
         load.wait()
 
-    def one_step(t, carry):
-        grid_ref[...] = scale * jnp.dot(
-            dft_ref[...], half_ref[t], precision=HIGHEST, preferred_element_type=jnp.float32
+    table = dft_ref[...]
+    high = table.astype(jnp.bfloat16)
+    low = (table - high.astype(jnp.float32)).astype(jnp.bfloat16)
+    table = jnp.concatenate([high, low], axis=0)
+    for t in range(steps):
+        both = jnp.dot(
+            table, half_ref[t].astype(jnp.bfloat16), preferred_element_type=jnp.float32
         )
+        grid_ref[t] = scale * (both[: 2 * NPIX] + both[2 * NPIX :])
+
+    def one_step(at, t, carry):
         for s in range(subs):
             row = off_ref[0, t, 0, s] - base
             col = off_ref[0, t, 1, s]
-            live = (s < cnt_ref[0, t]) & (row > -NPIX) & (row < rows)
+            live = (s < cnt_ref[0, t]) & (row < rows)
+            live = live & ((row > -NPIX) & (row < split) if at == 0 else row >= split)
 
             @pl.when(live)
             def _():
                 shift = col % 128
                 left = pl.multiple_of(col - shift, 128)
-                grid = jnp.where(lane // NPIX == s, grid_ref[...], 0.0)
+                grid = jnp.where(lane // NPIX == s, grid_ref[t], 0.0)
                 grid = pltpu.roll(grid, (shift + 128 - NPIX * s) % 128, 1)
                 down = (row + NPIX) % 8
                 top = pl.multiple_of(row + NPIX - down, 8)
@@ -301,10 +327,13 @@
 
         return carry
 
-    lax.fori_loop(0, steps, one_step, 0)
-    copy = pltpu.make_async_copy(tile_ref.at[:, pl.ds(NPIX, rows), :], out_ref.at[0], sem)
-    copy.start()
-    copy.wait()
+    lax.fori_loop(0, steps, functools.partial(one_step, 0), 0)
+    write(0).start()
+    clear(cuts[1], cuts[2])
+    lax.fori_loop(0, steps, functools.partial(one_step, 1), 0)
+    write(1).start()
+    write(0).wait()
+    write(1).wait()
 
 
 def tables(bands, steps, subs):
@@ -379,10 +408,10 @@
             pltpu.SMEM(counts.shape, jnp.int32),
             pltpu.VMEM(half.shape, f32),
             pltpu.VMEM(rows_dft.shape, f32),
-            pltpu.VMEM((2 * NPIX, subs * NPIX), f32),
+            pltpu.VMEM((steps, 2 * NPIX, subs * NPIX), f32),
             pltpu.VMEM((2, rows + 2 * NPIX, TILE), f32),
             pltpu.SemaphoreType.DMA((4,)),
-            dma,
+            pltpu.SemaphoreType.DMA((2,)),
         ],
         compiler_params=pltpu.CompilerParams(vmem_limit_bytes=VMEM_LIMIT),
     )(offsets, counts, half, rows_dft)

time: 21.7 us -> 21.2 us (0.977)
  Pallas kernels: 21.5 us -> 21 us
    pallas_call x1, Pallas kernels: 3.85 us -> 3.5 us  [body(): pl.pallas_call(functools.partial(place_kernel, (steps, subs, rows, TILE),...]
where the time goes in v4:
time: 21.2 us; the launch traced here: 21.1 us
  Pallas kernels  21 us (99%)
    pallas_call x1, Pallas kernels, body(): pl.pallas_call(functools.partial(image_kernel, (facets, bands, steps, sub...  17.5 us
    pallas_call x1, Pallas kernels, body(): pl.pallas_call(functools.partial(place_kernel, (steps, subs, rows, TILE),...  3.5 us

profile of v4, /device:TPU:0, one launch (start us, length us, event | category | flops | bytes accessed | tf_op | source)
XLA Modules:
  0.0 21.1 jit_solution(8980987237361999312)
XLA Ops:
  0.0 17.5 %shard_map.91.half_hbm = f32[4,64,128]{2,1,0:T(8,128)} custom-call(s32[4]{0:T(128)} %owner_hbm.1, f32[4,4,2,256]{3,2,1,0:T(2,128)} %uv_hbm.1, bf16[1,4,16,2,256]{4,3,2,1,0:T(2,128)(2,1)} %vis_hbm.1, bf16[1,4,4,2,1024]{4,3,2,1,0:T(2,128)(2,1)} %ate_hbm.1, f32[256,128]{1,0:T(8,128)} %constant.6.clone.dft_hbm, f32[32,128]{1,0:T(8,128)} %constant.7.clone.sel_hbm), custom_call_target="tpu_custom_call" | custom-call | tf_op jit(solution)/shard_map/pallas_call | solution.py:371
  17.6 3.5 %shard_map.92 = f32[1,2,256,2048]{3,2,1,0:T(8,128)} custom-call(s32[1,4,2,4]{3,2,1,0:T(2,128)} %off_hbm.1, s32[1,4]{1,0:T(1,128)} %cnt_hbm.1, f32[4,64,128]{2,1,0:T(8,128)} %shard_map.91.half_hbm, f32[64,64]{1,0:T(8,128)} %constant.8.clone.dft_hbm), custom_call_target="tpu_custom_call" | custom-call | tf_op jit(solution)/shard_map/pallas_call | solution.py:401
